TPU v7x, 32 devices: a whole 2x2x4 slice. The times are simulated.
32 devices in a mesh: dp: 4 (over y, core), sy: 4 (over z), sx: 2 (over x).
Axes of the slice: x: 2, y: 2, z: 4, core: 2. Of those that a mesh axis runs over, the one named last changes fastest.
Arguments:
- inputs: bfloat16 [4, 8, 32, 4, 512], P('dp', None, 'sy', 'sx'), may hold values from -6 to 6
- pre_activation: bfloat16 [4, 8, 32, 4, 512], P('dp', None, 'sy', 'sx'), may hold values from -6 to 6
- upstream: bfloat16 [4, 8, 32, 4, 512], P('dp', None, 'sy', 'sx'), may hold values from -6 to 6
- weight: bfloat16 [27, 512, 512], P(None, 'dp'), may hold values from -0.0546875 to 0.0546875
- first_moment: float32 [13824, 128], P(('dp', 'sy', 'sx')), may hold values from -4 to 4
- second_moment: float32 [13824, 128], P(('dp', 'sy', 'sx')), may hold values from 0.05 to 1
- hash_seed: int32 [], replicated, may hold values from 0 to 999999
- step_count: int32 [], replicated, may hold values from 1 to 29
Outputs:
- input_grad: bfloat16 [4, 8, 32, 4, 512], P('dp', None, 'sy', 'sx')
- new_first: float32 [13824, 128], P(('dp', 'sy', 'sx'))
- new_second: float32 [13824, 128], P(('dp', 'sy', 'sx'))
- scales: float32 [13824], P(('dp', 'sy', 'sx'))
All inputs are finite; a program needn't handle non-finite values.
Results may differ from a plain program's by a relative error of at most 0.004.
Values may be sent and summed in bfloat16 or wider, within the bound.
A program may use at most 128 MiB of HBM per device.

v0:
```python
import math

import jax
import jax.numpy as jnp
from jax import lax
from jax.sharding import PartitionSpec as P


def extended(cells, sides, width):
    for axis, dim in sides:
        count = lax.axis_size(axis)
        ends = count - 1
        head = lax.slice_in_dim(cells, 0, width, axis=dim)
        tail = lax.slice_in_dim(cells, cells.shape[dim] - width, cells.shape[dim], axis=dim)
        cells = jnp.concatenate(
            [
                lax.ppermute(tail, axis, [(i, (i + 1) % count) for i in range(ends)]),
                cells,
                lax.ppermute(head, axis, [((i + 1) % count, i) for i in range(ends)]),
            ],
            axis=dim,
        )
    return cells


def projection(hash_seed, rows_count, cols_count):
    row_ids = lax.broadcasted_iota(jnp.int32, (rows_count, cols_count), 0)
    col_ids = lax.broadcasted_iota(jnp.int32, (rows_count, cols_count), 1)
    mixed = (row_ids * cols_count + col_ids) * jnp.int32(-1640531535) + hash_seed * jnp.int32(
        668265263
    )
    mixed = mixed ^ lax.shift_right_logical(mixed, jnp.int32(15))
    mixed = mixed * jnp.int32(-2048144777)
    mixed = mixed ^ lax.shift_right_logical(mixed, jnp.int32(13))
    mixed = mixed * jnp.int32(-1028477379)
    mixed = mixed ^ lax.shift_right_logical(mixed, jnp.int32(16))
    level = (lax.shift_right_logical(mixed, jnp.int32(8)) & jnp.int32(65535)).astype(jnp.float32)
    return ((level + 0.5) * (2.0 / 65536.0) - 1.0) * math.sqrt(3.0 / cols_count)


def pad_time(volume):
    return jnp.pad(volume, ((1, 1), (0, 0), (0, 0), (0, 0)))


def windows(padded, stack_axis):
    frame_count = padded.shape[0] - 2
    height_count = padded.shape[1] - 2
    width_count = padded.shape[2] - 2
    channels = padded.shape[3]
    pieces = []
    for offset in range(27):
        along_t = offset // 9
        along_h = offset // 3 % 3
        along_w = offset % 3
        along_t, along_h, along_w = (2 - along_t, 2 - along_h, 2 - along_w)
        window_block = padded[
            along_t : along_t + frame_count,
            along_h : along_h + height_count,
            along_w : along_w + width_count,
        ]
        pieces.append(window_block.reshape(frame_count * height_count * width_count, channels))
    return jnp.stack(pieces, axis=stack_axis)


def body(
    inputs, pre_activation, upstream, weight, first_moment, second_moment, hash_seed, step_count
):
    source = inputs[0]
    frame_count, height_count, width_count, in_width = source.shape
    tokens_here = frame_count * height_count * width_count
    out_width = pre_activation.shape[-1]
    rank_width = first_moment.shape[1]
    rows_here = first_moment.shape[0]
    pre_value = pre_activation[0].astype(jnp.float32)
    upstream_value = upstream[0].astype(jnp.float32)
    sigmoid_value = jax.nn.sigmoid(pre_value)
    grad_pre = (upstream_value * sigmoid_value * (1.0 + pre_value * (1.0 - sigmoid_value))).astype(
        jnp.bfloat16
    )
    projector = projection(hash_seed, out_width, rank_width).astype(jnp.bfloat16)
    proj_grad = jnp.dot(
        grad_pre.reshape(tokens_here, out_width), projector, preferred_element_type=jnp.float32
    )
    proj_grad = proj_grad.astype(jnp.bfloat16)
    joined = jnp.concatenate(
        [grad_pre, proj_grad.reshape(frame_count, height_count, width_count, rank_width)], axis=3
    )
    joined = pad_time(extended(joined, (("sy", 1), ("sx", 2)), 1))
    grad_padded = joined[..., :out_width]
    proj_cols = windows(joined[..., out_width:], 1)
    flat_source = source.reshape(tokens_here, in_width)
    grad_cols = windows(grad_padded, 1)
    branch = jnp.einsum(
        "toc,oic->ti",
        grad_cols,
        lax.all_gather(weight, "dp", axis=1, tiled=True),
        preferred_element_type=jnp.float32,
    )
    input_grad = (upstream_value.reshape(tokens_here, in_width) + branch).astype(jnp.bfloat16)
    input_grad = input_grad.reshape(1, frame_count, height_count, width_count, in_width)
    product = jnp.einsum("tc,tor->cor", flat_source, proj_cols, preferred_element_type=jnp.float32)
    summed = lax.psum_scatter(
        product.reshape(rows_here * lax.axis_size(("dp", "sy", "sx")) // 27 * 27, rank_width),
        ("dp", "sy", "sx"),
        scatter_dimension=0,
        tiled=True,
    )
    token_total = tokens_here * lax.axis_size("dp") * lax.axis_size("sy") * lax.axis_size("sx")
    reduced = summed / math.sqrt(token_total)
    new_first = 0.9 * first_moment + 0.1 * reduced
    new_second = 0.999 * second_moment + 0.001 * reduced * reduced
    step_value = step_count.astype(jnp.float32)
    first_bias = 1.0 - jnp.power(jnp.float32(0.9), step_value)
    second_bias = 1.0 - jnp.power(jnp.float32(0.999), step_value)
    adapted = new_first / first_bias / (jnp.sqrt(new_second / second_bias) + 1e-08)
    scales = jnp.sqrt(jnp.mean(adapted * adapted, axis=1)) / jnp.sqrt(
        jnp.mean(reduced * reduced, axis=1) + 1e-06
    )
    return (input_grad, new_first, new_second, scales)


def solution(mesh):
    placed = (
        P("dp", None, "sy", "sx", None),
        P("dp", None, "sy", "sx", None),
        P("dp", None, "sy", "sx", None),
        P(None, "dp", None),
        P(("dp", "sy", "sx"), None),
        P(("dp", "sy", "sx"), None),
        P(),
        P(),
    )
    return jax.shard_map(
        body,
        mesh=mesh,
        in_specs=placed,
        out_specs=(
            P("dp", None, "sy", "sx", None),
            P(("dp", "sy", "sx"), None),
            P(("dp", "sy", "sx"), None),
            P(("dp", "sy", "sx")),
        ),
        check_vma=False,
    )
```

profile of v0, /device:TPU:0, one launch (start us, length us, event | category | flops | bytes accessed | tf_op | source)
XLA Modules:
  0.0 237.6 jit_solution(4700718251076712539)
XLA Ops:
  8.1 0.9 copy_convert_fusion.1
  9.0 1.0 copy_convert_fusion
  10.0 1.1 fusion.24
  13.0 4.9 %collective-permute-start = (bf16[8,1,2,640]{3,1,2,0:T(2,128)(2,1)S(1)}, bf16[8,1,2,640]{3,1,2,0:T(2,128)(2,1)S(1)}, u32[]{:S(2)}, u32[]{:S(2)}) collective-permute-start(bf16[8,1,2,640]{3,1,2,0:T(2,128)(2,1)S(1)} %get-tuple-element.64), channel_id=1, source_target_pairs={{0,2},{2,4},{4,6},{1,3},{3,5},{5,7},{8,10},{10,12},{12,14},{9,11},... | collective-permute-start | bytes 61448 | tf_op jit(solution)/shard_map/ppermute | solution.py:17
  18.0 1.3 collective-permute-start.1
  19.6 4.2 %collective-permute-done.1 = bf16[8,1,2,640]{3,1,2,0:T(2,128)(2,1)S(1)} collective-permute-done((bf16[8,1,2,640]{3,1,2,0:T(2,128)(2,1)S(1)}, bf16[8,1,2,640]{3,1,2,0:T(2,128)(2,1)S(1)}, u32[]{:S(2)}, u32[]{:S(2)}) %collective-permute-start.1) | collective-permute-done | bytes 20512 | tf_op jit(solution)/shard_map/ppermute | solution.py:19
  24.1 3.4 %collective-permute-start.2 = (bf16[8,10,1,640]{3,1,2,0:T(8,128)(2,1)S(1)}, bf16[8,10,1,640]{3,1,2,0:T(8,128)(2,1)S(1)}, u32[]{:S(2)}, u32[]{:S(2)}) collective-permute-start(bf16[8,10,1,640]{3,1,2,0:T(8,128)(2,1)S(1)} %get-tuple-element.55), channel_id=1, source_target_pairs={{0,1},{2,3},{4,5},{6,7},{8,9},{10,11},{12,13},{14,15},{16,17},{18,... | collective-permute-start | bytes 307208 | tf_op jit(solution)/shard_map/ppermute | solution.py:17
  27.5 1.3 collective-permute-start.3
  28.9 1.4 collective-permute-done.2
  30.3 4.4 %collective-permute-done.3 = bf16[8,10,1,640]{3,1,2,0:T(8,128)(2,1)S(1)} collective-permute-done((bf16[8,10,1,640]{3,1,2,0:T(8,128)(2,1)S(1)}, bf16[8,10,1,640]{3,1,2,0:T(8,128)(2,1)S(1)}, u32[]{:S(2)}, u32[]{:S(2)}) %collective-permute-start.3) | collective-permute-done | bytes 102432 | tf_op jit(solution)/shard_map/ppermute | solution.py:19
  36.5 4.0 %convolution_bitcast_fusion = f32[512,27,128]{0,2,1:T(8,128)} fusion(bf16[128,27,128]{2,0,1:T(8,128)(2,1)S(1)} %constant_dynamic-update-slice_fusion.26, bf16[128,512,1]{1,0,2:T(8,128)(2,1)S(1)} %reshape.79), kind=kOutput, calls=%fused_computation | convolution fusion | flops 452984832 | bytes 8093696 | tf_op jit(solution)/shard_map/tc,tor->cor/dot_general | solution.py:101
  40.5 10.3 %copy.82 = f32[512,27,128]{2,1,0:T(8,128)} copy(f32[512,27,128]{0,2,1:T(8,128)} %convolution_bitcast_fusion) | data formatting | bytes 14155776 | tf_op jit(solution)/shard_map/tc,tor->cor/dot_general | solution.py:101
  50.8 8.8 %reshape.71 = f32[13824,128]{1,0:T(8,128)} reshape(f32[512,27,128]{2,1,0:T(8,128)} %copy.82) | data formatting | bytes 14155776 | tf_op jit(solution)/shard_map/reshape | solution.py:103
  60.2 1.0 copy.37
  61.2 1.0 copy.38
  63.2 0.7 stack_reshape.170
  64.8 1.1 fusion.58
  66.6 1.1 copy.25
  72.7 0.7 stack_reshape.167
  86.3 0.7 stack_reshape.185
  87.1 1.0 constant_dynamic-update-slice_fusion.25
  88.0 1.0 constant_dynamic-update-slice_fusion.24
  89.0 0.9 constant_dynamic-update-slice_fusion.23
  89.9 0.9 constant_dynamic-update-slice_fusion.22
  90.9 0.9 constant_dynamic-update-slice_fusion.21
  91.8 0.9 constant_dynamic-update-slice_fusion.20
  92.7 0.9 constant_dynamic-update-slice_fusion.19
  93.6 0.9 constant_dynamic-update-slice_fusion.18
  94.6 0.9 constant_dynamic-update-slice_fusion.17
  95.5 0.9 constant_dynamic-update-slice_fusion.16
  96.4 0.9 constant_dynamic-update-slice_fusion.15
  97.3 0.9 constant_dynamic-update-slice_fusion.14
  98.3 0.9 constant_dynamic-update-slice_fusion.13
  99.2 1.1 fusion.29
  100.3 0.9 constant_dynamic-update-slice_fusion.12
  101.3 0.9 constant_dynamic-update-slice_fusion.11
  102.2 0.9 constant_dynamic-update-slice_fusion.10
  103.1 0.9 constant_dynamic-update-slice_fusion.9
  104.0 0.9 constant_dynamic-update-slice_fusion.8
  105.0 0.9 constant_dynamic-update-slice_fusion.7
  105.9 0.9 constant_dynamic-update-slice_fusion.6
  106.8 0.9 constant_dynamic-update-slice_fusion.5
  107.7 0.9 constant_dynamic-update-slice_fusion.4
  108.6 0.9 constant_dynamic-update-slice_fusion.3
  109.6 106.0 %reduce-scatter.2.cloned.1.call-done = f32[432,128]{1,0:T(8,128)} async-done(((f32[13824,128]{1,0:T(8,128)}), f32[432,128]{1,0:T(8,128)}) %reduce-scatter.2.cloned.1.call-update) | async-done | bytes 221200 | tf_op jit(solution)/shard_map/reduce_scatter | solution.py:102
  215.6 2.1 multiply_reduce_fusion.1
  218.3 10.2 %fusion.2 = bf16[128,512]{1,0:T(8,128)(2,1)} fusion(f32[128,512]{1,0:T(8,128)} %copy-done, bf16[128,27,512]{2,0,1:T(8,128)(2,1)S(1)} %constant_dynamic-update-slice_fusion, bf16[27,512,512]{2,1,0:T(8,128)(2,1)} %all-gather.2.cloned.1.call-done), kind=kOutput, calls=%fused_computation.6 | convolution fusion | flops 1812070400 | bytes 18087936 | tf_op jit(solution)/shard_map/toc,oic->ti/dot_general | solution.py:93
  228.5 1.6 reshape.70
  (139 shorter events, 24.1 us)
Async XLA Ops:
  8.0 207.6 %reduce-scatter.2.cloned.1.call-start = ((), (), s32[]{:S(2)}) async-start(), calls=%async_computation.2 | async-start | bytes 7299072 | tf_op jit(solution)/shard_map/reduce_scatter | solution.py:102
  9.0 19.8 %copy-start.4 = (bf16[1,8,8,2,512]{4,3,2,1,0:T(2,128)(2,1)S(1)}, bf16[1,8,8,2,512]{4,3,2,1,0:T(2,128)(2,1)}, u32[]{:S(2)}) copy-start(bf16[1,8,8,2,512]{4,3,2,1,0:T(2,128)(2,1)} %param.8) | copy-start | bytes 393220
  11.5 18.9 %copy-start = (f32[128,512]{1,0:T(8,128)}, f32[128,512]{1,0:T(8,128)S(1)}, u32[]{:S(2)}) copy-start(f32[128,512]{1,0:T(8,128)S(1)} %reshape.72) | copy-start | bytes 786436
  13.0 6.6 %collective-permute-start = (bf16[8,1,2,640]{3,1,2,0:T(2,128)(2,1)S(1)}, bf16[8,1,2,640]{3,1,2,0:T(2,128)(2,1)S(1)}, u32[]{:S(2)}, u32[]{:S(2)}) collective-permute-start(bf16[8,1,2,640]{3,1,2,0:T(2,128)(2,1)S(1)} %get-tuple-element.64), channel_id=1, source_target_pairs={{0,2},{2,4},{4,6},{1,3},{3,5},{5,7},{8,10},{10,12},{12,14},{9,11},... | collective-permute-start | bytes 61448 | tf_op jit(solution)/shard_map/ppermute | solution.py:17
  18.0 5.9 %collective-permute-start.1 = (bf16[8,1,2,640]{3,1,2,0:T(2,128)(2,1)S(1)}, bf16[8,1,2,640]{3,1,2,0:T(2,128)(2,1)S(1)}, u32[]{:S(2)}, u32[]{:S(2)}) collective-permute-start(bf16[8,1,2,640]{3,1,2,0:T(2,128)(2,1)S(1)} %get-tuple-element.65), channel_id=1, source_target_pairs={{2,0},{4,2},{6,4},{3,1},{5,3},{7,5},{10,8},{12,10},{14,12},{11,9},... | collective-permute-start | bytes 61448 | tf_op jit(solution)/shard_map/ppermute | solution.py:19
  24.1 6.2 %collective-permute-start.2 = (bf16[8,10,1,640]{3,1,2,0:T(8,128)(2,1)S(1)}, bf16[8,10,1,640]{3,1,2,0:T(8,128)(2,1)S(1)}, u32[]{:S(2)}, u32[]{:S(2)}) collective-permute-start(bf16[8,10,1,640]{3,1,2,0:T(8,128)(2,1)S(1)} %get-tuple-element.55), channel_id=1, source_target_pairs={{0,1},{2,3},{4,5},{6,7},{8,9},{10,11},{12,13},{14,15},{16,17},{18,... | collective-permute-start | bytes 307208 | tf_op jit(solution)/shard_map/ppermute | solution.py:17
  27.5 7.2 %collective-permute-start.3 = (bf16[8,10,1,640]{3,1,2,0:T(8,128)(2,1)S(1)}, bf16[8,10,1,640]{3,1,2,0:T(8,128)(2,1)S(1)}, u32[]{:S(2)}, u32[]{:S(2)}) collective-permute-start(bf16[8,10,1,640]{3,1,2,0:T(8,128)(2,1)S(1)} %get-tuple-element.56), channel_id=1, source_target_pairs={{1,0},{3,2},{5,4},{7,6},{9,8},{11,10},{13,12},{15,14},{17,16},{19,... | collective-permute-start | bytes 307208 | tf_op jit(solution)/shard_map/ppermute | solution.py:19
  59.7 158.6 %all-gather.2.cloned.1.call-start = ((), (), s32[]{:S(2)}) async-start(), calls=%async_computation.1 | async-start | bytes 17694720 | tf_op jit(solution)/shard_map/all_gather | solution.py:96
  87.1 22.5 %copy-start.1 = (bf16[128,1,512]{2,0,1:T(8,128)(2,1)S(1)}, bf16[128,1,512]{2,0,1:T(8,128)(2,1)}, u32[]{:S(2)}) copy-start(bf16[128,1,512]{2,0,1:T(8,128)(2,1)} %stack_reshape.183) | copy-start | bytes 393220
  87.1 22.5 %copy-start.2 = (bf16[128,1,512]{2,0,1:T(8,128)(2,1)S(1)}, bf16[128,1,512]{2,0,1:T(8,128)(2,1)}, u32[]{:S(2)}) copy-start(bf16[128,1,512]{2,0,1:T(8,128)(2,1)} %stack_reshape.184) | copy-start | bytes 393220
  88.0 21.6 %copy-start.3 = (bf16[128,1,512]{2,0,1:T(8,128)(2,1)S(1)}, bf16[128,1,512]{2,0,1:T(8,128)(2,1)}, u32[]{:S(2)}) copy-start(bf16[128,1,512]{2,0,1:T(8,128)(2,1)} %stack_reshape.185) | copy-start | bytes 393220
Sparse Core Ops, SparseCore 0:
  59.8 155.8 reduce-scatter.1
Sparse Core Ops, SparseCore 1:
  61.7 90.5 all-gather.1
where the time goes:
time: 239 us; the launch traced here: 238 us
  waiting for transfers between devices  117 us (49%)
  local copies, waits for them, and re-layouts  69.4 us (29%)
  between operations  17.7 us (7%)
  matrix products  14.7 us (6%)
  starting transfers between devices  11.2 us (5%)
  other arithmetic  7.78 us (3%)
    reduce_scatter x1, waiting for transfers between devices, body(): lax.psum_scatter(product.reshape(rows_here * lax.axis_size(('dp', 'sy', '...  106 us
    unnamed x61, local copies, waits for them, and re-layouts  21.6 us
    another operation x28, local copies, waits for them, and re-layouts, windows(): return jnp.stack(pieces, axis=stack_axis)  18.6 us
    dot_general x1, local copies, waits for them, and re-layouts, body(): jnp.einsum('tc,tor->cor', flat_source, proj_cols, preferred_element_type=...  10.3 us
    dot_general x1, matrix products, body(): jnp.einsum('toc,oic->ti', grad_cols, lax.all_gather(weight, 'dp', axis=1,...  10.2 us
    reshape x1, local copies, waits for them, and re-layouts, body(): product.reshape(rows_here * lax.axis_size(('dp', 'sy', 'sx')) // 27 * 27,...  8.79 us
    ppermute x2, waiting for transfers between devices, extended(): lax.ppermute(head, axis, [((i + 1) % count, i) for i in range(ends)])  8.64 us
    ppermute x2, starting transfers between devices, extended(): lax.ppermute(tail, axis, [(i, (i + 1) % count) for i in range(ends)])  8.33 us
  transfers between devices with their start and end apart: 6, of which 5 were waited for; matrix products, arithmetic and copies ran while one was open for 21% of the time, Pallas kernels for 0%

commit v1 on v0

--- a/solution.py
+++ b/solution.py
@@ -1,9 +1,16 @@
+import functools
 import math
 
 import jax
 import jax.numpy as jnp
+import ml_dtypes
+import numpy as np
 from jax import lax
+from jax.experimental import pallas as pl
+from jax.experimental.pallas import tpu as pltpu
 from jax.sharding import PartitionSpec as P
+
+MESH = pl.DeviceIdType.MESH
 
 
 def extended(cells, sides, width):
@@ -62,6 +69,20 @@
     return jnp.stack(pieces, axis=stack_axis)
 
 
+def update(summed, token_total, first_moment, second_moment, step_count):
+    reduced = summed / math.sqrt(token_total)
+    new_first = 0.9 * first_moment + 0.1 * reduced
+    new_second = 0.999 * second_moment + 0.001 * reduced * reduced
+    step_value = step_count.astype(jnp.float32)
+    first_bias = 1.0 - jnp.power(jnp.float32(0.9), step_value)
+    second_bias = 1.0 - jnp.power(jnp.float32(0.999), step_value)
+    adapted = new_first / first_bias / (jnp.sqrt(new_second / second_bias) + 1e-08)
+    scales = jnp.sqrt(jnp.mean(adapted * adapted, axis=1)) / jnp.sqrt(
+        jnp.mean(reduced * reduced, axis=1) + 1e-06
+    )
+    return (new_first, new_second, scales)
+
+
 def body(
     inputs, pre_activation, upstream, weight, first_moment, second_moment, hash_seed, step_count
 ):
@@ -106,17 +127,421 @@
         tiled=True,
     )
     token_total = tokens_here * lax.axis_size("dp") * lax.axis_size("sy") * lax.axis_size("sx")
-    reduced = summed / math.sqrt(token_total)
-    new_first = 0.9 * first_moment + 0.1 * reduced
-    new_second = 0.999 * second_moment + 0.001 * reduced * reduced
-    step_value = step_count.astype(jnp.float32)
-    first_bias = 1.0 - jnp.power(jnp.float32(0.9), step_value)
-    second_bias = 1.0 - jnp.power(jnp.float32(0.999), step_value)
-    adapted = new_first / first_bias / (jnp.sqrt(new_second / second_bias) + 1e-08)
-    scales = jnp.sqrt(jnp.mean(adapted * adapted, axis=1)) / jnp.sqrt(
-        jnp.mean(reduced * reduced, axis=1) + 1e-06
-    )
-    return (input_grad, new_first, new_second, scales)
+    return (input_grad, *update(summed, token_total, first_moment, second_moment, step_count))
+
+
+def tables(frames, high, wide, sy_count, sx_count, dp_count, chunk, channels):
+    cell = high * wide
+    own = frames * cell
+    pieces = []
+    offset = 0
+    for da in (-1, 0, 1):
+        for db in (-1, 0, 1):
+            if da == 0 and db == 0:
+                continue
+            rows = [0 if da < 0 else high - 1] if da else list(range(high))
+            cols = [0 if db < 0 else wide - 1] if db else list(range(wide))
+            spots = [(h, w) for h in rows for w in cols]
+            size = -(-frames * len(spots) // 16) * 16
+            pieces.append((da, db, spots, offset, size))
+            offset += size
+    edge = np.zeros((offset, own), np.float32)
+    shared = sx_count == 2
+    slots = {}
+    for h in range(high):
+        for w in range(wide):
+            slots[(h, w)] = len(slots)
+    for da, db, spots, start, _ in pieces:
+        for h, w in spots:
+            spot = (h if not da else (high if da < 0 else -1), w if not db else (wide if db < 0 else -1))
+            other = (spot[0], wide if spot[1] == -1 else -1)
+            if shared and db and other in slots:
+                slots[spot] = slots[other]
+            else:
+                slots[spot] = len(set(slots.values()))
+    span = -(-len(set(slots.values())) // 16) * 16
+    gather_own = np.zeros((frames * span, own), np.float32)
+    gather_halo = np.zeros((frames * span, offset), np.float32)
+    for t in range(frames):
+        for place in range(cell):
+            gather_own[t * span + place, t * cell + place] = 1
+        for da, db, spots, start, _ in pieces:
+            for n, (h, w) in enumerate(spots):
+                edge[start + t * len(spots) + n, t * cell + h * wide + w] = 1
+                spot = (h if not da else (high if da < 0 else -1), w if not db else (wide if db < 0 else -1))
+                gather_halo[t * span + slots[spot], start + t * len(spots) + n] = 1
+    select = np.zeros((2, 9 * cell, span), np.float32)
+    for side in range(2):
+        for j in range(9):
+            for h in range(high):
+                for w in range(wide):
+                    at = (h + 1 - j // 3, w + 1 - j % 3)
+                    if shared and at[1] == (-1 if side == 0 else wide):
+                        continue
+                    select[side, j * cell + h * wide + w, slots[at]] = 1
+    peers = sy_count * sx_count
+    ids = np.arange(peers * cell)
+    peer, inner = ids // cell, ids % cell
+    row = peer // sx_count * high + inner // wide
+    col = peer % sx_count * wide + inner % wide
+    shift = np.zeros((peers * cell, 9 * peers * cell), np.float32)
+    for j in range(9):
+        hit = (row[:, None] == row[None] + j // 3 - 1) & (col[:, None] == col[None] + j % 3 - 1)
+        shift[:, j * peers * cell : (j + 1) * peers * cell] = hit
+    group = np.zeros((2, channels, peers * 128), np.float32)
+    for part in range(2):
+        for d in range(dp_count):
+            for p in range(peers):
+                for c in range(chunk):
+                    group[part, (d * peers + p) * chunk + c, p * 128 + part * 64 + d * 16 + c] = 1
+    cast = [m.astype(ml_dtypes.bfloat16) for m in (edge, gather_own, gather_halo, select, shift, group)]
+    return pieces, span, cast
+
+
+def dot(left, right):
+    return jnp.dot(left, right, preferred_element_type=jnp.float32)
+
+
+def kernel(
+    sizes, pieces,
+    grad_ref, source_ref, upstream_ref, projector_ref, weight_hbm,
+    edge_ref, gather_own_ref, gather_halo_ref, select_ref, shift_ref, group_ref,
+    out_ref, reduced_ref,
+    weight, edges, halo, blocks, windows_buf, packed, packed_in, proj, proj_in,
+    shifted, parts, part_out, part_in, total, branch_in,
+    weight_sem, halo_send, halo_recv, pack_send, pack_recv, proj_send, proj_recv,
+    block_send, block_recv, part_send, part_recv, branch_send, branch_recv,
+):
+    dp, sy, sx, frames, cell, span = sizes
+    peers = sy * sx
+    half = frames // 2
+    frame = peers * cell
+    bf16 = jnp.bfloat16
+    d, a, b = lax.axis_index("dp"), lax.axis_index("sy"), lax.axis_index("sx")
+    me = a * sx + b
+
+    load = pltpu.make_async_copy(weight_hbm, weight, weight_sem)
+    load.start()
+
+    def peer_at(step):
+        other = (me + step) % peers
+        return other, (d, other // sx, other % sx)
+
+    def dp_at(step):
+        other = (d + step) % dp
+        return other, (other, a, b)
+
+    barrier = pltpu.get_barrier_semaphore()
+    for step in range(1, peers):
+        pl.semaphore_signal(barrier, inc=1, device_id=peer_at(step)[1], device_id_type=MESH)
+    for step in range(1, dp):
+        pl.semaphore_signal(barrier, inc=1, device_id=dp_at(step)[1], device_id_type=MESH)
+
+    edges[...] = dot(edge_ref[...], grad_ref[...]).astype(bf16)
+    proj[...] = dot(grad_ref[...], projector_ref[...]).astype(bf16).reshape(proj.shape)
+    pl.semaphore_wait(barrier, peers + dp - 2)
+
+    def halo_copy(k):
+        da, db, _, start, size = pieces[k]
+        to_a = jnp.clip(a + da, 0, sy - 1)
+        to_b = jnp.clip(b + db, 0, sx - 1)
+        return pltpu.make_async_remote_copy(
+            src_ref=edges.at[pl.ds(start, size)], dst_ref=halo.at[pl.ds(start, size)],
+            send_sem=halo_send.at[k], recv_sem=halo_recv.at[k],
+            device_id=(d, to_a, to_b), device_id_type=MESH,
+        )
+
+    def inside(at, count, move):
+        return (at + move >= 0) & (at + move < count)
+
+    for k, (da, db, _, start, size) in enumerate(pieces):
+        @pl.when(inside(a, sy, da) & inside(b, sx, db))
+        def _(k=k):
+            halo_copy(k).start()
+
+        @pl.when(jnp.logical_not(inside(a, sy, -da) & inside(b, sx, -db)))
+        def _(start=start, size=size):
+            halo[pl.ds(start, size), :] = jnp.zeros((size, halo.shape[1]), bf16)
+
+    mine = pl.ds(pl.multiple_of(me * cell, 16), cell)
+    proj_copies = []
+    for step in range(1, peers):
+        proj_copies.append(pltpu.make_async_remote_copy(
+            src_ref=proj, dst_ref=proj_in.at[:, mine, :],
+            send_sem=proj_send.at[step], recv_sem=proj_recv.at[step],
+            device_id=peer_at(step)[1], device_id_type=MESH,
+        ))
+        proj_copies[-1].start()
+    split = half * cell
+    spread = dot(source_ref[:split, :], group_ref[0]) + dot(source_ref[split:, :], group_ref[1])
+    spread = spread.astype(bf16)
+    for p in range(peers):
+        packed[p] = spread[:, p * 128 : (p + 1) * 128].reshape(half, cell, 128)
+    pack_copies = []
+    for step in range(1, peers):
+        other, place = peer_at(step)
+        pack_copies.append(pltpu.make_async_remote_copy(
+            src_ref=packed.at[other], dst_ref=packed_in.at[:, mine, :],
+            send_sem=pack_send.at[step], recv_sem=pack_recv.at[step],
+            device_id=place, device_id_type=MESH,
+        ))
+        pack_copies[-1].start()
+    packed_in[:, mine, :] = packed[me]
+    proj_in[:, mine, :] = proj[...]
+
+    for k, (da, db, _, start, size) in enumerate(pieces):
+        @pl.when(inside(a, sy, -da) & inside(b, sx, -db))
+        def _(k=k):
+            halo_copy(k).wait_recv()
+
+    block = dot(gather_own_ref[...], grad_ref[...]) + dot(gather_halo_ref[...], halo[...])
+    blocks[d] = block.astype(bf16).reshape(frames, span, block.shape[1])
+
+    def flip(at, bit):
+        return at + bit * (1 - 2 * ((at // bit) % 2))
+
+    block_copies = []
+    bits = []
+    bit = dp // 2
+    while bit:
+        bits.append(bit)
+        bit //= 2
+
+    def send_block(bit, mask, wait_first):
+        if wait_first is not None:
+            wait_first.wait_recv()
+        slot = d
+        for one in bits:
+            if mask & one:
+                slot = flip(slot, one)
+        n = len(block_copies)
+        block_copies.append(pltpu.make_async_remote_copy(
+            src_ref=blocks.at[slot], dst_ref=blocks.at[slot],
+            send_sem=block_send.at[n], recv_sem=block_recv.at[n],
+            device_id=(flip(d, bit), a, b), device_id_type=MESH,
+        ))
+        block_copies[-1].start()
+        return block_copies[-1]
+
+    arrivals = {}
+    for bit in bits:
+        arrivals[bit] = send_block(bit, 0, None)
+
+    for copy in pack_copies + proj_copies:
+        copy.wait_recv()
+
+    for ot in (-1, 1):
+        last = frames - 1 if ot > 0 else 0
+        for c in range(dp):
+            shifted[c, pl.ds(9 * (ot + 1), 9), :, pl.ds(last * frame, frame)] = jnp.zeros(
+                (9, 16, frame), bf16
+            )
+    for n in range(half):
+        turned = packed_in[n].astype(jnp.float32).T.astype(bf16)
+        moved = dot(turned, shift_ref[...]).astype(bf16)
+        for j in range(9):
+            piece = moved[:, j * frame : (j + 1) * frame]
+            for part in range(2):
+                for ot in (-1, 0, 1):
+                    at = part * half + n - ot
+                    if 0 <= at < frames:
+                        for c in range(dp):
+                            low = part * 64 + c * 16
+                            shifted[c, 9 * (ot + 1) + j, :, pl.ds(at * frame, frame)] = piece[
+                                low : low + 16
+                            ]
+
+    held = [0]
+    received = {}
+    for bit in bits:
+        fresh = []
+        for mask in held:
+            if mask == 0:
+                copy = arrivals[bit]
+            else:
+                source = received.pop(mask) if mask in received else None
+                copy = send_block(bit, mask, source)
+            received[mask | bit] = copy
+            fresh.append(mask | bit)
+        held += fresh
+
+    whole_proj = proj_in[...].reshape(frames * frame, proj_in.shape[2])
+    for c in range(dp):
+        part = dot(shifted[c].reshape(27 * 16, frames * frame), whole_proj)
+        parts[c] = part
+        part_out[c] = part.astype(bf16)
+    part_copies = []
+    for step in range(1, dp):
+        other, place = dp_at(step)
+        part_copies.append(pltpu.make_async_remote_copy(
+            src_ref=part_out.at[other], dst_ref=part_in.at[step],
+            send_sem=part_send.at[step], recv_sem=part_recv.at[step],
+            device_id=place, device_id_type=MESH,
+        ))
+        part_copies[-1].start()
+
+    for copy in received.values():
+        copy.wait_recv()
+    depth = windows_buf.shape[-1]
+    edge_zero = jnp.zeros((9, dp, cell, depth), bf16)
+    windows_buf[:, :, 0] = edge_zero
+    windows_buf[:, :, frames + 1] = edge_zero
+
+    def build(n, carry):
+        s, t = n // frames, n % frames
+        found = dot(select_ref[...], blocks[s, t]).astype(bf16)
+        windows_buf[:, s, t + 1] = found.reshape(9, cell, depth)
+        return carry
+
+    lax.fori_loop(0, dp * frames, build, 0)
+    load.wait()
+    total[...] = jnp.zeros(total.shape, jnp.float32)
+
+    def tap_step(j, carry):
+        value = total[...]
+        for t in range(3):
+            rows = windows_buf[j, :, 2 - t : 2 - t + frames].reshape(dp * frames * cell, depth)
+            value = value + lax.dot_general(
+                rows, weight[t * 9 + j], (((1,), (1,)), ((), ())),
+                preferred_element_type=jnp.float32,
+            )
+        total[...] = value
+        return carry
+
+    lax.fori_loop(0, 9, tap_step, 0)
+    tokens = frames * cell
+    branch_copies = []
+    for step in range(1, dp):
+        other, place = dp_at(step)
+        branch_copies.append(pltpu.make_async_remote_copy(
+            src_ref=total.at[pl.ds(pl.multiple_of(other * tokens, 16), tokens)],
+            dst_ref=branch_in.at[d],
+            send_sem=branch_send.at[step], recv_sem=branch_recv.at[step],
+            device_id=place, device_id_type=MESH,
+        ))
+        branch_copies[-1].start()
+    branch_in[d] = total[pl.ds(pl.multiple_of(d * tokens, 16), tokens), :]
+
+    for copy in part_copies:
+        copy.wait_recv()
+    summed = parts[d]
+    for step in range(1, dp):
+        summed = summed + part_in[step].astype(jnp.float32)
+    reduced_ref[...] = summed
+    for copy in branch_copies:
+        copy.wait_recv()
+    width = branch_in.shape[2]
+    for c in range(dp):
+        cols = slice(c * width, (c + 1) * width)
+        out_ref[:, cols] = (upstream_ref[:, cols].astype(jnp.float32) + branch_in[c]).astype(bf16)
+
+    for k, (da, db, _, start, size) in enumerate(pieces):
+        @pl.when(inside(a, sy, da) & inside(b, sx, db))
+        def _(k=k):
+            halo_copy(k).wait_send()
+    for copy in proj_copies + pack_copies + block_copies + part_copies + branch_copies:
+        copy.wait_send()
+
+
+def fused_body(
+    inputs, pre_activation, upstream, weight, first_moment, second_moment, hash_seed, step_count
+):
+    source = inputs[0]
+    frames, high, wide, channels = source.shape
+    depth = pre_activation.shape[-1]
+    rank = first_moment.shape[1]
+    dp, sy, sx = (lax.axis_size(name) for name in ("dp", "sy", "sx"))
+    cell, peers = high * wide, sy * sx
+    tokens, frame = frames * cell, peers * cell
+    chunk = first_moment.shape[0] // 27
+    ci = weight.shape[1]
+    pieces, span, consts = tables(frames, high, wide, sy, sx, dp, chunk, channels)
+    edge, gather_own, gather_halo, select, shift, group = consts
+    side = (lax.axis_index("sx") > 0).astype(jnp.int32)
+    select = lax.dynamic_index_in_dim(jnp.asarray(select), side, 0, keepdims=False)
+    pre_value = pre_activation[0].astype(jnp.float32)
+    upstream_value = upstream[0].astype(jnp.float32)
+    sigmoid_value = jax.nn.sigmoid(pre_value)
+    grad_pre = (upstream_value * sigmoid_value * (1.0 + pre_value * (1.0 - sigmoid_value))).astype(
+        jnp.bfloat16
+    )
+    projector = projection(hash_seed, depth, rank).astype(jnp.bfloat16)
+    halo_rows = edge.shape[0]
+    bf16, f32 = jnp.bfloat16, jnp.float32
+    dma = pltpu.SemaphoreType.DMA
+    vmem = pl.BlockSpec(memory_space=pltpu.VMEM)
+    input_grad, summed = pl.pallas_call(
+        functools.partial(kernel, (dp, sy, sx, frames, cell, span), pieces),
+        out_shape=(
+            jax.ShapeDtypeStruct((tokens, channels), bf16),
+            jax.ShapeDtypeStruct((27 * 16, rank), f32),
+        ),
+        in_specs=[vmem] * 4 + [pl.BlockSpec(memory_space=pl.ANY)] + [vmem] * 6,
+        out_specs=(vmem, vmem),
+        scratch_shapes=[
+            pltpu.VMEM(weight.shape, bf16),
+            pltpu.VMEM((halo_rows, depth), bf16),
+            pltpu.VMEM((halo_rows, depth), bf16),
+            pltpu.VMEM((dp, frames, span, depth), bf16),
+            pltpu.VMEM((9, dp, frames + 2, cell, depth), bf16),
+            pltpu.VMEM((peers, frames // 2, cell, 128), bf16),
+            pltpu.VMEM((frames // 2, frame, 128), bf16),
+            pltpu.VMEM((frames, cell, rank), bf16),
+            pltpu.VMEM((frames, frame, rank), bf16),
+            pltpu.VMEM((dp, 27, 16, frames * frame), bf16),
+            pltpu.VMEM((dp, 27 * 16, rank), f32),
+            pltpu.VMEM((dp, 27 * 16, rank), bf16),
+            pltpu.VMEM((dp, 27 * 16, rank), bf16),
+            pltpu.VMEM((dp * tokens, ci), f32),
+            pltpu.VMEM((dp, tokens, ci), f32),
+            dma,
+            dma((8,)), dma((8,)),
+            dma((peers,)), dma((peers,)),
+            dma((peers,)), dma((peers,)),
+            dma((dp,)), dma((dp,)),
+            dma((dp,)), dma((dp,)),
+            dma((dp,)), dma((dp,)),
+        ],
+        compiler_params=pltpu.CompilerParams(
+            collective_id=0, has_side_effects=True, vmem_limit_bytes=48 * 1024 * 1024
+        ),
+    )(
+        grad_pre.reshape(tokens, depth),
+        source.reshape(tokens, channels),
+        upstream[0].reshape(tokens, channels),
+        projector,
+        weight,
+        jnp.asarray(edge), jnp.asarray(gather_own), jnp.asarray(gather_halo), select,
+        jnp.asarray(shift), jnp.asarray(group),
+    )
+    input_grad = input_grad.reshape(1, frames, high, wide, channels)
+    summed = summed.reshape(27, 16, rank)[:, :chunk].transpose(1, 0, 2).reshape(27 * chunk, rank)
+    return (input_grad, *update(summed, tokens * dp * peers, first_moment, second_moment, step_count))
+
+
+def fits(mesh, args):
+    dp, sy, sx = mesh.shape["dp"], mesh.shape["sy"], mesh.shape["sx"]
+    _, frames, high, wide, channels = args[0].shape
+    rank = args[4].shape[1]
+    high, wide, peers = high // sy, wide // sx, sy * sx
+    cell = high * wide
+    frame = cell * peers
+    chunk = args[4].shape[0] // 27 // (dp * peers)
+    depth = args[3].shape[2]
+    return (
+        dp == 4
+        and args[0].shape[0] == dp
+        and frames % 2 == 0
+        and cell % 16 == 0
+        and frame % 128 == 0
+        and chunk <= 16
+        and rank % 128 == 0
+        and channels % (128 * dp) == 0
+        and depth % 128 == 0
+        and 18 * frame * frame + 512 * channels * peers < 6 * 2**20
+        and 2 * 27 * (64 * frames * frame + channels // dp * depth) < 16 * 2**20
+        and 18 * dp * (frames + 2) * cell * depth < 12 * 2**20
+    )
 
 
 def solution(mesh):
@@ -130,8 +555,12 @@
         P(),
         P(),
     )
-    return jax.shard_map(
-        body,
+    def run(*args):
+        return mapped(fused_body if fits(mesh, args) else body)(*args)
+
+    def mapped(part):
+      return jax.shard_map(
+        part,
         mesh=mesh,
         in_specs=placed,
         out_specs=(
@@ -142,3 +571,5 @@
         ),
         check_vma=False,
     )
+
+    return run

time: 239 us -> 48.8 us (0.20)
  waiting for transfers between devices: 117 us -> 0 us
  local copies, waits for them, and re-layouts: 69.4 us -> 9.92 us
  Pallas kernels: 0 us -> 33.8 us
  between operations: 17.7 us -> 2.12 us
  matrix products: 14.7 us -> 0 us
  starting transfers between devices: 11.2 us -> 0 us
  other arithmetic: 7.78 us -> 1.99 us
    reduce_scatter x1 -> x0, waiting for transfers between devices: 106 us -> none  [body(): lax.psum_scatter(product.reshape(rows_here * lax.axis_size(('dp', 'sy', '...]
    pallas_call x0 -> x1, Pallas kernels: none -> 33.8 us  [fused_body(): pl.pallas_call(functools.partial(kernel, (dp, sy, sx, frames, cell, span)...]
    another operation x29 -> x1, local copies, waits for them, and re-layouts: 18.6 us -> 0.96 us  [fused_body(): source.reshape(tokens, channels)]
    unnamed x61 -> x14, local copies, waits for them, and re-layouts: 21.6 us -> 5.12 us
    dot_general x3 -> x0, matrix products: 14.7 us -> none  [the longest x1 10.2 us: body(): jnp.einsum('toc,oic->ti', grad_cols, lax.all_gather(weight, 'dp', axis=1,...]
    ppermute x4 -> x0, starting transfers between devices: 10.9 us -> none  [the longest x2 8.33 us: extended(): lax.ppermute(tail, axis, [(i, (i + 1) % count) for i in range(ends)])]
    ppermute x4 -> x0, waiting for transfers between devices: 10.4 us -> none  [the longest x2 8.64 us: extended(): lax.ppermute(head, axis, [((i + 1) % count, i) for i in range(ends)])]
    dot_general x1 -> x0, local copies, waits for them, and re-layouts: 10.3 us -> none  [body(): jnp.einsum('tc,tor->cor', flat_source, proj_cols, preferred_element_type=...]
  transfers between devices with their start and end apart: 6 -> 0, of which waited for: 5 -> 0; matrix products, arithmetic and copies ran while one was open for 21% -> 0% of each run, Pallas kernels for 0% -> 0%
where the time goes in v1:
time: 48.8 us; the launch traced here: 47.8 us
  Pallas kernels  33.8 us (69%)
  local copies, waits for them, and re-layouts  9.92 us (20%)
  between operations  2.12 us (4%)
  other arithmetic  1.99 us (4%)
    pallas_call x1, Pallas kernels, fused_body(): pl.pallas_call(functools.partial(kernel, (dp, sy, sx, frames, cell, span)...  33.8 us
    unnamed x14, local copies, waits for them, and re-layouts  5.12 us

profile of v1, /device:TPU:0, one launch (start us, length us, event | category | flops | bytes accessed | tf_op | source)
XLA Modules:
  0.0 47.8 jit_solution(13682889002827306001)
XLA Ops:
  0.6 0.8 %dynamic-slice_bitcast_fusion.select_ref = bf16[144,32]{1,0:T(8,128)(2,1)S(1)} fusion(bf16[2,144,32]{2,1,0:T(8,128)(2,1)} %constant.80.clone, s32[]{:T(128)S(6)} %select_n.4), kind=kLoop, calls=%fused_computation.22 | loop fusion | bytes 18436 | tf_op jit(solution)/shard_map/jit(dynamic_index_in_dim)/squeeze | solution.py:461
  1.4 1.0 %squeeze.8.upstream_ref = bf16[128,512]{1,0:T(8,128)(2,1)S(1)} reshape(bf16[1,8,8,2,512]{4,3,2,1,0:T(2,128)(2,1)} %param.16) | data formatting | bytes 262144 | tf_op jit(solution)/shard_map/squeeze | solution.py:463
  2.4 0.9 %reshape.43 = f32[128,512]{1,0:T(8,128)S(1)} reshape(bf16[1,8,8,2,512]{4,3,2,1,0:T(2,128)(2,1)} %param.15) | data formatting | bytes 393216 | tf_op jit(solution)/shard_map/convert_element_type | solution.py:462
  3.3 0.1 multiply_convert_fusion.grad_ref
  4.1 0.2 fusion.9.projector_ref
  4.3 1.0 %reshape_squeeze.4.source_ref = bf16[128,512]{1,0:T(8,128)(2,1)S(1)} reshape(bf16[1,8,8,2,512]{4,3,2,1,0:T(2,128)(2,1)} %param.14) | data formatting | bytes 262144 | tf_op jit(solution)/shard_map/reshape;squeeze | solution.py:510
  5.3 0.0 copy-start
  5.3 1.6 %copy-done = bf16[2,512,1024]{2,1,0:T(8,128)(2,1)S(1)} copy-done((bf16[2,512,1024]{2,1,0:T(8,128)(2,1)S(1)}, bf16[2,512,1024]{2,1,0:T(8,128)(2,1)}, u32[]{:S(2)}) %copy-start) | copy-done | bytes 2097176
  6.9 0.0 copy-start.1
  6.9 1.0 %copy-done.1 = bf16[128,1152]{1,0:T(8,128)(2,1)S(1)} copy-done((bf16[128,1152]{1,0:T(8,128)(2,1)S(1)}, bf16[128,1152]{1,0:T(8,128)(2,1)}, u32[]{:S(2)}) %copy-start.1) | copy-done | bytes 294936
  7.9 0.0 copy-start.2
  7.9 0.9 %copy-done.2 = bf16[256,224]{1,0:T(8,128)(2,1)S(1)} copy-done((bf16[256,224]{1,0:T(8,128)(2,1)S(1)}, bf16[256,224]{1,0:T(8,128)(2,1)}, u32[]{:S(2)}) %copy-start.2) | copy-done | bytes 114712
  8.8 0.0 copy-start.3
  8.8 0.8 %copy-done.3 = bf16[256,128]{1,0:T(8,128)(2,1)S(1)} copy-done((bf16[256,128]{1,0:T(8,128)(2,1)S(1)}, bf16[256,128]{1,0:T(8,128)(2,1)}, u32[]{:S(2)}) %copy-start.3) | copy-done | bytes 65560
  9.6 0.0 copy-start.4
  9.6 0.8 %copy-done.4 = bf16[224,128]{1,0:T(8,128)(2,1)S(1)} copy-done((bf16[224,128]{1,0:T(8,128)(2,1)S(1)}, bf16[224,128]{1,0:T(8,128)(2,1)}, u32[]{:S(2)}) %copy-start.4) | copy-done | bytes 57368
  10.4 0.0 copy-start.5
  10.4 0.0 copy-start.6
  10.4 33.8 %shard_map.165 = (bf16[128,512]{1,0:T(8,128)(2,1)S(1)}, f32[432,128]{1,0:T(8,128)S(1)}) custom-call(bf16[128,512]{1,0:T(8,128)(2,1)S(1)} %multiply_convert_fusion.grad_ref, bf16[128,512]{1,0:T(8,128)(2,1)S(1)} %reshape_squeeze.4.source_ref, bf16[128,512]{1,0:T(8,128)(2,1)S(1)} %squeeze.8.upstream_ref, bf16[512,128]{1,0:T(8,128)(2,1)S(1)} %fusion.9.projector_ref, ...), custom_call_target="tpu_custom_call" | custom-call | tf_op jit(solution)/shard_map/pallas_call | solution.py:473
  44.2 0.1 multiply_reduce_fusion
  44.4 0.1 copy.26
  44.5 0.1 copy.25
  45.3 0.0 copy-done.5
  45.3 0.0 copy-done.6
  45.4 0.9 %multiply_reduce_fusion.1 = (f32[432]{0:T(512)S(1)}, f32[432,128]{1,0:T(8,128)}, f32[432,128]{1,0:T(8,128)}) fusion(f32[]{:T(128)S(6)} %sub.17, f32[]{:T(128)S(6)} %sub.16, f32[432,128]{1,0:T(8,128)S(1)} %mul.139, f32[432,128]{1,0:T(8,128)S(1)} %copy-done.5, f32[432,128]{1,0:T(8,128)S(1)} %mul.131, f32[432,128]{1,0:T(8,128)S(1)} %copy-done.6), kind=kLoop, calls=%fused_computation.17 | loop fusion | flops 552528 | bytes 1328840 | tf_op jit(solution)/shard_map/reduce_sum | solution.py:80
  46.2 0.1 reshape.48
  46.3 0.1 copy.22
  46.4 0.1 sqrt.14
  46.5 0.6 %sqrt_multiply_fusion = f32[432]{0:T(512)} fusion(f32[432]{0:T(512)S(1)} %sqrt.14, f32[432]{0:T(512)S(1)} %get-tuple-element.8), kind=kLoop, calls=%fused_computation.24 | loop fusion | flops 864 | bytes 5184 | tf_op jit(solution)/shard_map/div | solution.py:80
  47.1 0.7 %reshape.42 = bf16[1,8,8,2,512]{4,3,2,1,0:T(2,128)(2,1)} reshape(bf16[128,512]{1,0:T(8,128)(2,1)S(1)} %get-tuple-element.6) | data formatting | bytes 262144 | tf_op jit(solution)/shard_map/reshape | solution.py:517
  (4 shorter events, 0.0 us)
Async XLA Ops:
  5.3 1.6 %copy-start = (bf16[2,512,1024]{2,1,0:T(8,128)(2,1)S(1)}, bf16[2,512,1024]{2,1,0:T(8,128)(2,1)}, u32[]{:S(2)}) copy-start(bf16[2,512,1024]{2,1,0:T(8,128)(2,1)} %constant.85.clone.group_ref) | copy-start | bytes 6291460
  6.9 1.0 %copy-start.1 = (bf16[128,1152]{1,0:T(8,128)(2,1)S(1)}, bf16[128,1152]{1,0:T(8,128)(2,1)}, u32[]{:S(2)}) copy-start(bf16[128,1152]{1,0:T(8,128)(2,1)} %constant.84.clone.shift_ref) | copy-start | bytes 884740
  7.9 0.9 %copy-start.2 = (bf16[256,224]{1,0:T(8,128)(2,1)S(1)}, bf16[256,224]{1,0:T(8,128)(2,1)}, u32[]{:S(2)}) copy-start(bf16[256,224]{1,0:T(8,128)(2,1)} %constant.83.clone.gather_halo_ref) | copy-start | bytes 344068
  8.8 0.8 %copy-start.3 = (bf16[256,128]{1,0:T(8,128)(2,1)S(1)}, bf16[256,128]{1,0:T(8,128)(2,1)}, u32[]{:S(2)}) copy-start(bf16[256,128]{1,0:T(8,128)(2,1)} %constant.82.clone.gather_own_ref) | copy-start | bytes 196612
  9.6 0.8 %copy-start.4 = (bf16[224,128]{1,0:T(8,128)(2,1)S(1)}, bf16[224,128]{1,0:T(8,128)(2,1)}, u32[]{:S(2)}) copy-start(bf16[224,128]{1,0:T(8,128)(2,1)} %constant.81.clone.edge_ref) | copy-start | bytes 172036
  10.4 34.9 %copy-start.5 = (f32[432,128]{1,0:T(8,128)S(1)}, f32[432,128]{1,0:T(8,128)}, u32[]{:S(2)}) copy-start(f32[432,128]{1,0:T(8,128)} %param.19) | copy-start | bytes 663556
  10.4 34.9 %copy-start.6 = (f32[432,128]{1,0:T(8,128)S(1)}, f32[432,128]{1,0:T(8,128)}, u32[]{:S(2)}) copy-start(f32[432,128]{1,0:T(8,128)} %param.18) | copy-start | bytes 663556

commit v2 on v1

--- a/solution.py
+++ b/solution.py
@@ -170,7 +170,7 @@
                 edge[start + t * len(spots) + n, t * cell + h * wide + w] = 1
                 spot = (h if not da else (high if da < 0 else -1), w if not db else (wide if db < 0 else -1))
                 gather_halo[t * span + slots[spot], start + t * len(spots) + n] = 1
-    select = np.zeros((2, 9 * cell, span), np.float32)
+    select = np.zeros((2, 9, frames, cell, frames, span), np.float32)
     for side in range(2):
         for j in range(9):
             for h in range(high):
@@ -178,7 +178,13 @@
                     at = (h + 1 - j // 3, w + 1 - j % 3)
                     if shared and at[1] == (-1 if side == 0 else wide):
                         continue
-                    select[side, j * cell + h * wide + w, slots[at]] = 1
+                    for t in range(frames):
+                        select[side, j, t, h * wide + w, t, slots[at]] = 1
+    select = select.reshape(2, 9 * frames * cell, frames * span)
+    order = np.zeros((chunk * 27, 27 * 16), np.float32)
+    for c in range(chunk):
+        for tap in range(27):
+            order[c * 27 + tap, tap * 16 + c] = 1
     peers = sy_count * sx_count
     ids = np.arange(peers * cell)
     peer, inner = ids // cell, ids % cell
@@ -194,7 +200,7 @@
             for p in range(peers):
                 for c in range(chunk):
                     group[part, (d * peers + p) * chunk + c, p * 128 + part * 64 + d * 16 + c] = 1
-    cast = [m.astype(ml_dtypes.bfloat16) for m in (edge, gather_own, gather_halo, select, shift, group)]
+    cast = [m.astype(ml_dtypes.bfloat16) for m in (edge, gather_own, gather_halo, select, shift, group, order)]
     return pieces, span, cast
 
 
@@ -204,12 +210,15 @@
 
 def kernel(
     sizes, pieces,
-    grad_ref, source_ref, upstream_ref, projector_ref, weight_hbm,
-    edge_ref, gather_own_ref, gather_halo_ref, select_ref, shift_ref, group_ref,
-    out_ref, reduced_ref,
-    weight, edges, halo, blocks, windows_buf, packed, packed_in, proj, proj_in,
+    pre_ref, source_in, upstream_in, projector_ref, bias_ref, weight_hbm, first_hbm, second_hbm,
+    edge_hbm, own_hbm, halo_hbm, select_hbm, shift_hbm, group_hbm, order_hbm,
+    out_ref, first_out, second_out, scales_out,
+    grad_ref, source_ref, upstream_ref,
+    weight, first, second, edge_ref, gather_own_ref, gather_halo_ref, select_ref, shift_ref,
+    group_ref, order_ref,
+    edges, halo, blocks, windows_buf, packed, packed_in, proj, proj_in,
     shifted, parts, part_out, part_in, total, branch_in,
-    weight_sem, halo_send, halo_recv, pack_send, pack_recv, proj_send, proj_recv,
+    load_sem, halo_send, halo_recv, pack_send, pack_recv, proj_send, proj_recv,
     block_send, block_recv, part_send, part_recv, branch_send, branch_recv,
 ):
     dp, sy, sx, frames, cell, span = sizes
@@ -220,8 +229,26 @@
     d, a, b = lax.axis_index("dp"), lax.axis_index("sy"), lax.axis_index("sx")
     me = a * sx + b
 
-    load = pltpu.make_async_copy(weight_hbm, weight, weight_sem)
-    load.start()
+    side = jnp.minimum(b, 1)
+    loads = [
+        pltpu.make_async_copy(source, target, load_sem.at[n])
+        for n, (source, target) in enumerate(
+            (
+                (edge_hbm, edge_ref),
+                (group_hbm, group_ref),
+                (own_hbm, gather_own_ref),
+                (halo_hbm, gather_halo_ref),
+                (shift_hbm, shift_ref),
+                (select_hbm.at[side], select_ref),
+                (weight_hbm, weight),
+                (order_hbm, order_ref),
+                (first_hbm, first),
+                (second_hbm, second),
+            )
+        )
+    ]
+    for load in loads:
+        load.start()
 
     def peer_at(step):
         other = (me + step) % peers
@@ -237,8 +264,17 @@
     for step in range(1, dp):
         pl.semaphore_signal(barrier, inc=1, device_id=dp_at(step)[1], device_id_type=MESH)
 
+    wide_shape = upstream_ref.shape
+    upstream_value = upstream_in[...].astype(jnp.float32).reshape(wide_shape)
+    upstream_ref[...] = upstream_value
+    pre_value = pre_ref[...].astype(jnp.float32).reshape(wide_shape)
+    sigmoid_value = jax.nn.sigmoid(pre_value)
+    grad_ref[...] = (
+        upstream_value * sigmoid_value * (1.0 + pre_value * (1.0 - sigmoid_value))
+    ).astype(bf16)
+    proj[...] = dot(grad_ref[...], projector_ref[...]).astype(bf16).reshape(proj.shape)
+    loads[0].wait()
     edges[...] = dot(edge_ref[...], grad_ref[...]).astype(bf16)
-    proj[...] = dot(grad_ref[...], projector_ref[...]).astype(bf16).reshape(proj.shape)
     pl.semaphore_wait(barrier, peers + dp - 2)
 
     def halo_copy(k):
@@ -272,6 +308,8 @@
             device_id=peer_at(step)[1], device_id_type=MESH,
         ))
         proj_copies[-1].start()
+    source_ref[...] = source_in[...].astype(jnp.float32).reshape(source_ref.shape).astype(bf16)
+    loads[1].wait()
     split = half * cell
     spread = dot(source_ref[:split, :], group_ref[0]) + dot(source_ref[split:, :], group_ref[1])
     spread = spread.astype(bf16)
@@ -294,26 +332,26 @@
         def _(k=k):
             halo_copy(k).wait_recv()
 
+    loads[2].wait()
+    loads[3].wait()
     block = dot(gather_own_ref[...], grad_ref[...]) + dot(gather_halo_ref[...], halo[...])
     blocks[d] = block.astype(bf16).reshape(frames, span, block.shape[1])
 
     def flip(at, bit):
         return at + bit * (1 - 2 * ((at // bit) % 2))
 
+    def masked(mask):
+        at = d
+        for one in (2, 1):
+            if mask & one:
+                at = flip(at, one)
+        return at
+
     block_copies = []
-    bits = []
-    bit = dp // 2
-    while bit:
-        bits.append(bit)
-        bit //= 2
-
     def send_block(bit, mask, wait_first):
         if wait_first is not None:
             wait_first.wait_recv()
-        slot = d
-        for one in bits:
-            if mask & one:
-                slot = flip(slot, one)
+        slot = masked(mask)
         n = len(block_copies)
         block_copies.append(pltpu.make_async_remote_copy(
             src_ref=blocks.at[slot], dst_ref=blocks.at[slot],
@@ -324,7 +362,7 @@
         return block_copies[-1]
 
     arrivals = {}
-    for bit in bits:
+    for bit in (2, 1):
         arrivals[bit] = send_block(bit, 0, None)
 
     for copy in pack_copies + proj_copies:
@@ -336,6 +374,7 @@
             shifted[c, pl.ds(9 * (ot + 1), 9), :, pl.ds(last * frame, frame)] = jnp.zeros(
                 (9, 16, frame), bf16
             )
+    loads[4].wait()
     for n in range(half):
         turned = packed_in[n].astype(jnp.float32).T.astype(bf16)
         moved = dot(turned, shift_ref[...]).astype(bf16)
@@ -351,20 +390,6 @@
                                 low : low + 16
                             ]
 
-    held = [0]
-    received = {}
-    for bit in bits:
-        fresh = []
-        for mask in held:
-            if mask == 0:
-                copy = arrivals[bit]
-            else:
-                source = received.pop(mask) if mask in received else None
-                copy = send_block(bit, mask, source)
-            received[mask | bit] = copy
-            fresh.append(mask | bit)
-        held += fresh
-
     whole_proj = proj_in[...].reshape(frames * frame, proj_in.shape[2])
     for c in range(dp):
         part = dot(shifted[c].reshape(27 * 16, frames * frame), whole_proj)
@@ -380,60 +405,88 @@
         ))
         part_copies[-1].start()
 
-    for copy in received.values():
-        copy.wait_recv()
     depth = windows_buf.shape[-1]
+    tokens = frames * cell
+    loads[5].wait()
     edge_zero = jnp.zeros((9, dp, cell, depth), bf16)
     windows_buf[:, :, 0] = edge_zero
     windows_buf[:, :, frames + 1] = edge_zero
 
-    def build(n, carry):
-        s, t = n // frames, n % frames
-        found = dot(select_ref[...], blocks[s, t]).astype(bf16)
-        windows_buf[:, s, t + 1] = found.reshape(9, cell, depth)
-        return carry
-
-    lax.fori_loop(0, dp * frames, build, 0)
-    load.wait()
-    total[...] = jnp.zeros(total.shape, jnp.float32)
-
-    def tap_step(j, carry):
-        value = total[...]
-        for t in range(3):
-            rows = windows_buf[j, :, 2 - t : 2 - t + frames].reshape(dp * frames * cell, depth)
-            value = value + lax.dot_general(
-                rows, weight[t * 9 + j], (((1,), (1,)), ((), ())),
-                preferred_element_type=jnp.float32,
-            )
-        total[...] = value
-        return carry
-
-    lax.fori_loop(0, 9, tap_step, 0)
-    tokens = frames * cell
+    def build(mask):
+        rows = blocks[masked(mask)].reshape(frames * span, depth)
+        found = dot(select_ref[...], rows).astype(bf16)
+        windows_buf[:, mask, 1 : frames + 1] = found.reshape(9, frames, cell, depth)
+
+    def convolve(mask):
+        pair = slice(mask, mask + 2)
+        total[pair] = jnp.zeros((2, tokens, total.shape[2]), jnp.float32)
+
+        def tap_step(j, carry):
+            value = total[pair].reshape(2 * tokens, total.shape[2])
+            for t in range(3):
+                rows = windows_buf[j, pair, 2 - t : 2 - t + frames].reshape(2 * tokens, depth)
+                value = value + lax.dot_general(
+                    rows, weight[t * 9 + j], (((1,), (1,)), ((), ())),
+                    preferred_element_type=jnp.float32,
+                )
+            total[pair] = value.reshape(2, tokens, total.shape[2])
+            return carry
+
+        lax.fori_loop(0, 9, tap_step, 0)
+
     branch_copies = []
-    for step in range(1, dp):
-        other, place = dp_at(step)
+
+    def send_branch(mask):
         branch_copies.append(pltpu.make_async_remote_copy(
-            src_ref=total.at[pl.ds(pl.multiple_of(other * tokens, 16), tokens)],
-            dst_ref=branch_in.at[d],
-            send_sem=branch_send.at[step], recv_sem=branch_recv.at[step],
-            device_id=place, device_id_type=MESH,
+            src_ref=total.at[mask], dst_ref=branch_in.at[d],
+            send_sem=branch_send.at[mask], recv_sem=branch_recv.at[mask],
+            device_id=(masked(mask), a, b), device_id_type=MESH,
         ))
         branch_copies[-1].start()
-    branch_in[d] = total[pl.ds(pl.multiple_of(d * tokens, 16), tokens), :]
-
+
+    build(0)
+    arrivals[1].wait_recv()
+    build(1)
+    onward = send_block(1, 2, arrivals[2])
+    loads[6].wait()
+    convolve(0)
+    send_branch(1)
+    build(2)
+    onward.wait_recv()
+    build(3)
+    convolve(2)
+    send_branch(3)
+    send_branch(2)
+    branch_in[d] = total[0]
+
+    for load in loads[7:]:
+        load.wait()
     for copy in part_copies:
         copy.wait_recv()
     summed = parts[d]
     for step in range(1, dp):
         summed = summed + part_in[step].astype(jnp.float32)
-    reduced_ref[...] = summed
+    ordered = 0.0
+    for _ in range(3):
+        piece = summed.astype(bf16)
+        summed = summed - piece.astype(jnp.float32)
+        ordered = ordered + dot(order_ref[...], piece)
+    reduced = ordered / math.sqrt(tokens * dp * peers)
+    new_first = 0.9 * first[...] + 0.1 * reduced
+    new_second = 0.999 * second[...] + 0.001 * reduced * reduced
+    first_out[...] = new_first
+    second_out[...] = new_second
+    adapted = new_first / bias_ref[0] / (jnp.sqrt(new_second / bias_ref[1]) + 1e-08)
+    scales_out[...] = jnp.sqrt(jnp.mean(adapted * adapted, axis=1, keepdims=True)) / jnp.sqrt(
+        jnp.mean(reduced * reduced, axis=1, keepdims=True) + 1e-06
+    )
     for copy in branch_copies:
         copy.wait_recv()
     width = branch_in.shape[2]
     for c in range(dp):
         cols = slice(c * width, (c + 1) * width)
-        out_ref[:, cols] = (upstream_ref[:, cols].astype(jnp.float32) + branch_in[c]).astype(bf16)
+        value = upstream_ref[:, cols] + branch_in[c]
+        out_ref[:, :, cols] = value.reshape(*out_ref.shape[:2], width).astype(bf16)
 
     for k, (da, db, _, start, size) in enumerate(pieces):
         @pl.when(inside(a, sy, da) & inside(b, sx, db))
@@ -456,30 +509,39 @@
     chunk = first_moment.shape[0] // 27
     ci = weight.shape[1]
     pieces, span, consts = tables(frames, high, wide, sy, sx, dp, chunk, channels)
-    edge, gather_own, gather_halo, select, shift, group = consts
-    side = (lax.axis_index("sx") > 0).astype(jnp.int32)
-    select = lax.dynamic_index_in_dim(jnp.asarray(select), side, 0, keepdims=False)
-    pre_value = pre_activation[0].astype(jnp.float32)
-    upstream_value = upstream[0].astype(jnp.float32)
-    sigmoid_value = jax.nn.sigmoid(pre_value)
-    grad_pre = (upstream_value * sigmoid_value * (1.0 + pre_value * (1.0 - sigmoid_value))).astype(
-        jnp.bfloat16
-    )
+    edge, gather_own, gather_halo, select, shift, group, order = consts
+    step_value = step_count.astype(jnp.float32)
+    biases = 1.0 - jnp.power(jnp.asarray([0.9, 0.999], jnp.float32), step_value)
     projector = projection(hash_seed, depth, rank).astype(jnp.bfloat16)
     halo_rows = edge.shape[0]
     bf16, f32 = jnp.bfloat16, jnp.float32
     dma = pltpu.SemaphoreType.DMA
     vmem = pl.BlockSpec(memory_space=pltpu.VMEM)
-    input_grad, summed = pl.pallas_call(
+    hbm = pl.BlockSpec(memory_space=pl.ANY)
+    input_grad, new_first, new_second, scales = pl.pallas_call(
         functools.partial(kernel, (dp, sy, sx, frames, cell, span), pieces),
         out_shape=(
-            jax.ShapeDtypeStruct((tokens, channels), bf16),
-            jax.ShapeDtypeStruct((27 * 16, rank), f32),
+            jax.ShapeDtypeStruct((frames * high, wide, channels), bf16),
+            jax.ShapeDtypeStruct(first_moment.shape, f32),
+            jax.ShapeDtypeStruct(first_moment.shape, f32),
+            jax.ShapeDtypeStruct((first_moment.shape[0], 1), f32),
         ),
-        in_specs=[vmem] * 4 + [pl.BlockSpec(memory_space=pl.ANY)] + [vmem] * 6,
-        out_specs=(vmem, vmem),
+        in_specs=[vmem] * 4 + [pl.BlockSpec(memory_space=pltpu.SMEM)] + [hbm] * 10,
+        out_specs=(vmem,) * 4,
         scratch_shapes=[
+            pltpu.VMEM((tokens, depth), bf16),
+            pltpu.VMEM((tokens, channels), bf16),
+            pltpu.VMEM((tokens, channels), f32),
             pltpu.VMEM(weight.shape, bf16),
+            pltpu.VMEM(first_moment.shape, f32),
+            pltpu.VMEM(first_moment.shape, f32),
+            pltpu.VMEM(edge.shape, bf16),
+            pltpu.VMEM(gather_own.shape, bf16),
+            pltpu.VMEM(gather_halo.shape, bf16),
+            pltpu.VMEM(select.shape[1:], bf16),
+            pltpu.VMEM(shift.shape, bf16),
+            pltpu.VMEM(group.shape, bf16),
+            pltpu.VMEM(order.shape, bf16),
             pltpu.VMEM((halo_rows, depth), bf16),
             pltpu.VMEM((halo_rows, depth), bf16),
             pltpu.VMEM((dp, frames, span, depth), bf16),
@@ -492,9 +554,9 @@
             pltpu.VMEM((dp, 27 * 16, rank), f32),
             pltpu.VMEM((dp, 27 * 16, rank), bf16),
             pltpu.VMEM((dp, 27 * 16, rank), bf16),
-            pltpu.VMEM((dp * tokens, ci), f32),
             pltpu.VMEM((dp, tokens, ci), f32),
-            dma,
+            pltpu.VMEM((dp, tokens, ci), f32),
+            dma((10,)),
             dma((8,)), dma((8,)),
             dma((peers,)), dma((peers,)),
             dma((peers,)), dma((peers,)),
@@ -506,17 +568,18 @@
             collective_id=0, has_side_effects=True, vmem_limit_bytes=48 * 1024 * 1024
         ),
     )(
-        grad_pre.reshape(tokens, depth),
-        source.reshape(tokens, channels),
-        upstream[0].reshape(tokens, channels),
+        pre_activation[0].reshape(frames * high, wide, depth),
+        source.reshape(frames * high, wide, channels),
+        upstream[0].reshape(frames * high, wide, channels),
         projector,
+        biases,
         weight,
-        jnp.asarray(edge), jnp.asarray(gather_own), jnp.asarray(gather_halo), select,
-        jnp.asarray(shift), jnp.asarray(group),
+        first_moment,
+        second_moment,
+        *(jnp.asarray(m) for m in consts),
     )
     input_grad = input_grad.reshape(1, frames, high, wide, channels)
-    summed = summed.reshape(27, 16, rank)[:, :chunk].transpose(1, 0, 2).reshape(27 * chunk, rank)
-    return (input_grad, *update(summed, tokens * dp * peers, first_moment, second_moment, step_count))
+    return input_grad, new_first, new_second, scales.reshape(first_moment.shape[0])
 
 
 def fits(mesh, args):
@@ -533,6 +596,7 @@
         and args[0].shape[0] == dp
         and frames % 2 == 0
         and cell % 16 == 0
+        and high * frames % 8 == 0
         and frame % 128 == 0
         and chunk <= 16
         and rank % 128 == 0
@@ -559,7 +623,7 @@
         return mapped(fused_body if fits(mesh, args) else body)(*args)
 
     def mapped(part):
-      return jax.shard_map(
+        return jax.shard_map(
         part,
         mesh=mesh,
         in_specs=placed,

time: 48.8 us -> 51.4 us (1.053)
  local copies, waits for them, and re-layouts: 9.92 us -> 14 us
    unnamed x14 -> x27, local copies, waits for them, and re-layouts: 5.12 us -> 14 us
    squeeze x2 -> x0, local copies, waits for them, and re-layouts: 1.74 us -> none  [the longest x1 0.96 us: fused_body(): upstream_value = upstream[0].astype(jnp.float32)]
    reduce_sum x2 -> x0, other arithmetic: 1.03 us -> none  [the longest x1 0.88 us: update(): jnp.mean(adapted * adapted, axis=1)]
    another operation x1 -> x0, local copies, waits for them, and re-layouts: 0.96 us -> none  [fused_body(): source.reshape(tokens, channels)]
    convert_element_type x1 -> x0, local copies, waits for them, and re-layouts: 0.94 us -> none  [fused_body(): pre_value = pre_activation[0].astype(jnp.float32)]
    pallas_call x0 -> x1, other arithmetic: none -> 0.73 us  [fused_body(): pl.pallas_call(functools.partial(kernel, (dp, sy, sx, frames, cell, span)...]
    reshape x1 -> x0, local copies, waits for them, and re-layouts: 0.71 us -> none  [fused_body(): input_grad = input_grad.reshape(1, frames, high, wide, channels)]
    sub x0 -> x1, other arithmetic: none -> 0.68 us  [fused_body(): biases = 1.0 - jnp.power(jnp.asarray([0.9, 0.999], jnp.float32), step_value)]
where the time goes in v2:
time: 51.4 us; the launch traced here: 50.9 us
  Pallas kernels  33.3 us (65%)
  local copies, waits for them, and re-layouts  14 us (27%)
  between operations  1.97 us (4%)
  other arithmetic  1.65 us (3%)
    pallas_call x1, Pallas kernels, fused_body(): pl.pallas_call(functools.partial(kernel, (dp, sy, sx, frames, cell, span)...  33.3 us
    unnamed x27, local copies, waits for them, and re-layouts  14 us

profile of v2, /device:TPU:0, one launch (start us, length us, event | category | flops | bytes accessed | tf_op | source)
XLA Modules:
  0.0 50.9 jit_solution(12643553600929680542)
XLA Ops:
  1.9 0.7 %power_subtract_fusion.bias_ref = f32[2]{0:T(128)S(1)} fusion(f32[2]{0:T(128)} %constant.47.clone, f32[]{:T(128)S(6)} %convert_element_type.11), kind=kLoop, calls=%fused_computation.14 | loop fusion | flops 2 | bytes 20 | tf_op jit(solution)/shard_map/sub | solution.py:514
  2.6 0.2 fusion.9.projector_ref
  2.9 0.0 copy-start
  2.9 1.6 %copy-done = bf16[2,512,1024]{2,1,0:T(8,128)(2,1)S(1)} copy-done((bf16[2,512,1024]{2,1,0:T(8,128)(2,1)S(1)}, bf16[2,512,1024]{2,1,0:T(8,128)(2,1)}, u32[]{:S(2)}) %copy-start) | copy-done | bytes 2097176
  4.5 0.0 copy-start.1
  4.5 1.3 %copy-done.1 = bf16[2,1152,256]{2,1,0:T(8,128)(2,1)S(1)} copy-done((bf16[2,1152,256]{2,1,0:T(8,128)(2,1)S(1)}, bf16[2,1152,256]{2,1,0:T(8,128)(2,1)}, u32[]{:S(2)}) %copy-start.1) | copy-done | bytes 1179672
  5.7 0.0 copy-start.2
  5.7 1.0 %copy-done.2 = bf16[432,432]{1,0:T(8,128)(2,1)S(1)} copy-done((bf16[432,432]{1,0:T(8,128)(2,1)S(1)}, bf16[432,432]{1,0:T(8,128)(2,1)}, u32[]{:S(2)}) %copy-start.2) | copy-done | bytes 373272
  6.7 0.0 copy-start.3
  6.7 1.0 %copy-done.3 = bf16[128,1152]{1,0:T(8,128)(2,1)S(1)} copy-done((bf16[128,1152]{1,0:T(8,128)(2,1)S(1)}, bf16[128,1152]{1,0:T(8,128)(2,1)}, u32[]{:S(2)}) %copy-start.3) | copy-done | bytes 294936
  7.7 0.0 copy-start.4
  7.7 0.9 %copy-done.4 = f32[432,128]{1,0:T(8,128)S(1)} copy-done((f32[432,128]{1,0:T(8,128)S(1)}, f32[432,128]{1,0:T(8,128)}, u32[]{:S(2)}) %copy-start.4) | copy-done | bytes 221208
  8.6 0.0 copy-start.5
  8.6 0.9 %copy-done.5 = f32[432,128]{1,0:T(8,128)S(1)} copy-done((f32[432,128]{1,0:T(8,128)S(1)}, f32[432,128]{1,0:T(8,128)}, u32[]{:S(2)}) %copy-start.5) | copy-done | bytes 221208
  9.6 0.0 copy-start.6
  9.6 0.9 %copy-done.6 = bf16[1,8,8,2,512]{4,3,2,1,0:T(2,128)(2,1)S(1)} copy-done((bf16[1,8,8,2,512]{4,3,2,1,0:T(2,128)(2,1)S(1)}, bf16[1,8,8,2,512]{4,3,2,1,0:T(2,128)(2,1)}, u32[]{:S(2)}) %copy-start.6) | copy-done | bytes 131096
  10.5 0.0 copy-start.7
  10.5 0.9 %copy-done.7 = bf16[1,8,8,2,512]{4,3,2,1,0:T(2,128)(2,1)S(1)} copy-done((bf16[1,8,8,2,512]{4,3,2,1,0:T(2,128)(2,1)S(1)}, bf16[1,8,8,2,512]{4,3,2,1,0:T(2,128)(2,1)}, u32[]{:S(2)}) %copy-start.7) | copy-done | bytes 131096
  11.4 0.0 copy-start.8
  11.4 0.9 %copy-done.8 = bf16[1,8,8,2,512]{4,3,2,1,0:T(2,128)(2,1)S(1)} copy-done((bf16[1,8,8,2,512]{4,3,2,1,0:T(2,128)(2,1)S(1)}, bf16[1,8,8,2,512]{4,3,2,1,0:T(2,128)(2,1)}, u32[]{:S(2)}) %copy-start.8) | copy-done | bytes 131096
  12.3 0.0 copy-start.9
  12.3 0.9 %copy-done.9 = bf16[256,224]{1,0:T(8,128)(2,1)S(1)} copy-done((bf16[256,224]{1,0:T(8,128)(2,1)S(1)}, bf16[256,224]{1,0:T(8,128)(2,1)}, u32[]{:S(2)}) %copy-start.9) | copy-done | bytes 114712
  13.2 0.0 copy-start.10
  13.2 0.8 %copy-done.10 = bf16[256,128]{1,0:T(8,128)(2,1)S(1)} copy-done((bf16[256,128]{1,0:T(8,128)(2,1)S(1)}, bf16[256,128]{1,0:T(8,128)(2,1)}, u32[]{:S(2)}) %copy-start.10) | copy-done | bytes 65560
  14.0 0.0 copy-start.11
  14.0 0.8 %copy-done.11 = bf16[224,128]{1,0:T(8,128)(2,1)S(1)} copy-done((bf16[224,128]{1,0:T(8,128)(2,1)S(1)}, bf16[224,128]{1,0:T(8,128)(2,1)}, u32[]{:S(2)}) %copy-start.11) | copy-done | bytes 57368
  14.8 33.3 %shard_map.183 = (bf16[64,2,512]{2,1,0:T(2,128)(2,1)S(1)}, f32[432,128]{1,0:T(8,128)S(1)}, f32[432,128]{1,0:T(8,128)S(1)}, f32[432,1]{1,0:T(8,128)S(1)}) custom-call(bf16[64,2,512]{2,1,0:T(2,128)(2,1)S(1)} %bitcast.4, bf16[64,2,512]{2,1,0:T(2,128)(2,1)S(1)} %bitcast.5, bf16[64,2,512]{2,1,0:T(2,128)(2,1)S(1)} %bitcast.6, ...), custom_call_target="tpu_custom_call" | custom-call | tf_op jit(solution)/shard_map/pallas_call | solution.py:521
  48.1 0.7 %reduce = f32[432]{0:T(512)} reduce(f32[432,1]{1,0:T(8,128)S(1)} %get-tuple-element.11, f32[]{:T(128)} %constant.60), dimensions={1}, to_apply=%get-tuple-element.11.reduce_sub_computation | reduce | bytes 3460 | tf_op jit(solution)/shard_map/pallas_call | solution.py:521
  48.8 0.7 %copy.25 = bf16[1,8,8,2,512]{4,3,2,1,0:T(2,128)(2,1)} copy(bf16[1,8,8,2,512]{4,3,2,1,0:T(2,128)(2,1)S(1)} %bitcast.7) | data formatting | bytes 262144
  49.5 0.7 %copy.26 = f32[432,128]{1,0:T(8,128)} copy(f32[432,128]{1,0:T(8,128)S(1)} %get-tuple-element.17) | data formatting | bytes 442368
  50.2 0.7 %copy.27 = f32[432,128]{1,0:T(8,128)} copy(f32[432,128]{1,0:T(8,128)S(1)} %get-tuple-element.18) | data formatting | bytes 442368
  (1 shorter events, 0.0 us)
Async XLA Ops:
  2.9 1.6 %copy-start = (bf16[2,512,1024]{2,1,0:T(8,128)(2,1)S(1)}, bf16[2,512,1024]{2,1,0:T(8,128)(2,1)}, u32[]{:S(2)}) copy-start(bf16[2,512,1024]{2,1,0:T(8,128)(2,1)} %constant.53.clone.group_hbm) | copy-start | bytes 6291460
  4.5 1.3 %copy-start.1 = (bf16[2,1152,256]{2,1,0:T(8,128)(2,1)S(1)}, bf16[2,1152,256]{2,1,0:T(8,128)(2,1)}, u32[]{:S(2)}) copy-start(bf16[2,1152,256]{2,1,0:T(8,128)(2,1)} %constant.51.clone.select_hbm) | copy-start | bytes 3538948
  5.7 1.0 %copy-start.2 = (bf16[432,432]{1,0:T(8,128)(2,1)S(1)}, bf16[432,432]{1,0:T(8,128)(2,1)}, u32[]{:S(2)}) copy-start(bf16[432,432]{1,0:T(8,128)(2,1)} %constant.54.clone.order_hbm) | copy-start | bytes 1119748
  6.7 1.0 %copy-start.3 = (bf16[128,1152]{1,0:T(8,128)(2,1)S(1)}, bf16[128,1152]{1,0:T(8,128)(2,1)}, u32[]{:S(2)}) copy-start(bf16[128,1152]{1,0:T(8,128)(2,1)} %constant.52.clone.shift_hbm) | copy-start | bytes 884740
  7.7 0.9 %copy-start.4 = (f32[432,128]{1,0:T(8,128)S(1)}, f32[432,128]{1,0:T(8,128)}, u32[]{:S(2)}) copy-start(f32[432,128]{1,0:T(8,128)} %first_hbm.1) | copy-start | bytes 663556
  8.6 0.9 %copy-start.5 = (f32[432,128]{1,0:T(8,128)S(1)}, f32[432,128]{1,0:T(8,128)}, u32[]{:S(2)}) copy-start(f32[432,128]{1,0:T(8,128)} %second_hbm.1) | copy-start | bytes 663556
  9.6 0.9 %copy-start.6 = (bf16[1,8,8,2,512]{4,3,2,1,0:T(2,128)(2,1)S(1)}, bf16[1,8,8,2,512]{4,3,2,1,0:T(2,128)(2,1)}, u32[]{:S(2)}) copy-start(bf16[1,8,8,2,512]{4,3,2,1,0:T(2,128)(2,1)} %param.17) | copy-start | bytes 393220
  10.5 0.9 %copy-start.7 = (bf16[1,8,8,2,512]{4,3,2,1,0:T(2,128)(2,1)S(1)}, bf16[1,8,8,2,512]{4,3,2,1,0:T(2,128)(2,1)}, u32[]{:S(2)}) copy-start(bf16[1,8,8,2,512]{4,3,2,1,0:T(2,128)(2,1)} %param.16) | copy-start | bytes 393220
  11.4 0.9 %copy-start.8 = (bf16[1,8,8,2,512]{4,3,2,1,0:T(2,128)(2,1)S(1)}, bf16[1,8,8,2,512]{4,3,2,1,0:T(2,128)(2,1)}, u32[]{:S(2)}) copy-start(bf16[1,8,8,2,512]{4,3,2,1,0:T(2,128)(2,1)} %param.18) | copy-start | bytes 393220
  12.3 0.9 %copy-start.9 = (bf16[256,224]{1,0:T(8,128)(2,1)S(1)}, bf16[256,224]{1,0:T(8,128)(2,1)}, u32[]{:S(2)}) copy-start(bf16[256,224]{1,0:T(8,128)(2,1)} %constant.50.clone.halo_hbm) | copy-start | bytes 344068
  13.2 0.8 %copy-start.10 = (bf16[256,128]{1,0:T(8,128)(2,1)S(1)}, bf16[256,128]{1,0:T(8,128)(2,1)}, u32[]{:S(2)}) copy-start(bf16[256,128]{1,0:T(8,128)(2,1)} %constant.49.clone.own_hbm) | copy-start | bytes 196612
  14.0 0.8 %copy-start.11 = (bf16[224,128]{1,0:T(8,128)(2,1)S(1)}, bf16[224,128]{1,0:T(8,128)(2,1)}, u32[]{:S(2)}) copy-start(bf16[224,128]{1,0:T(8,128)(2,1)} %constant.48.clone.edge_hbm) | copy-start | bytes 172036
